TPU v7x, 32 devices: a whole 2x2x4 slice. The times are simulated.
32 devices in a mesh: grp: 4 (over z), dev: 8 (over y, x, core).
Axes of the slice: x: 2, y: 2, z: 4, core: 2. Of those that a mesh axis runs over, the one named last changes fastest.
Arguments:
- tracer: float32 [72, 16, 4096], P(None, None, ('grp', 'dev')), may hold values from -6 to 6
- metric: float32 [4096], P(('grp', 'dev')), may hold values from 0.5 to 2
- coef: float32 [72, 65536], P(None, ('grp', 'dev')), may hold values from 0.02 to 601
- nbr_slot: int32 [4, 4096], P(None, ('grp', 'dev')), may hold values from 0 to 559, as said below
- edge_flip: int32 [4, 4096], P(None, ('grp', 'dev')), may hold values from 0 to 1, as said below
- send_slot: int32 [1536], P(('grp', 'dev')), may hold values from 0 to 511, as said below
- span_slot: int32 [16, 4096], P(None, ('grp', 'dev')), may hold values from 0 to 16383, as said below
Outputs:
- mixed: float32 [72, 16, 4096], P(None, None, ('grp', 'dev'))
Inputs may be any that keep to these rules, and one draw needn't show every extreme that they name: `nbr_slot`: entries below 512 name an edge of an element of the same device as s * 128 + e; larger ones name the neighbouring devices' buffer entries in the order of the edge table. Each element edge meets exactly one other edge, both ways. `edge_flip`: symmetric over the two sides of a shared edge. `send_slot`: each entry is an own edge s * 128 + e'. For each device, 16 own edges whose neighbours lie on device (g + 1, v), 16 for (g - 1, v), 8 for (g, v + 1), 8 for (g, v - 1), in the order the receiving edge table expects. `span_slot`: within each group along dev the values form a permutation of 0 to 16383, and every device holds exactly 256 columns whose value lies in each range r * 2048 to (r + 1) * 2048 - 1.
All inputs are finite; a program needn't handle non-finite values.
Results may differ from a plain program's by a relative error of at most 0.0003.
Values sent between devices are 32-bit elements; how exact they have to be, the bound alone decides.
A program may use at most 64 MiB of HBM per device.

v0:
```python
import functools

import jax
import jax.numpy as jnp
import numpy as np
from jax import lax
from jax.experimental import pallas as pl
from jax.experimental.pallas import tpu as pltpu
from jax.sharding import PartitionSpec as P

PENALTY = 10.0
HYPER = 0.0001
LANES = 128
MESH = pl.DeviceIdType.MESH
F32 = jnp.float32
BF16 = jnp.bfloat16
I32 = jnp.int32

EDGE_POINT = [[0, 1, 2, 3], [3, 7, 11, 15], [12, 13, 14, 15], [0, 4, 8, 12]]
EDGE_ROWS = [(0, 16, 1, 0), (16, 16, -1, 0), (32, 8, 0, 1), (40, 8, 0, -1)]


def gll_laplacian():
    gll_nodes = np.array([-1.0, -1.0 / np.sqrt(5.0), 1.0 / np.sqrt(5.0), 1.0])
    weights = np.array([1.0 / 6.0, 5.0 / 6.0, 5.0 / 6.0, 1.0 / 6.0])
    lambdas = np.ones(4)
    for jdx in range(4):
        for kdx in range(4):
            if kdx != jdx:
                lambdas[jdx] = lambdas[jdx] / (gll_nodes[jdx] - gll_nodes[kdx])
    derivative = np.zeros((4, 4))
    for idx in range(4):
        for jdx in range(4):
            if idx != jdx:
                derivative[idx, jdx] = (
                    lambdas[jdx] / lambdas[idx] / (gll_nodes[idx] - gll_nodes[jdx])
                )
        derivative[idx, idx] = -np.sum(derivative[idx])
    stiffness = -(derivative.T * weights[None, :] @ derivative) / weights[:, None]
    identity = np.eye(4)
    return np.kron(stiffness, identity) + np.kron(identity, stiffness)


def iota(shape, dim):
    return lax.broadcasted_iota(I32, shape, dim)


def one_hot(cond):
    return jnp.where(cond, 1.0, 0.0).astype(BF16)


def halves(value):
    hi = value.astype(BF16)
    lo = (value - hi.astype(F32)).astype(BF16)
    return hi, lo


def pick(value, lanes):
    return jnp.take_along_axis(value, lanes, axis=1, mode="promise_in_bounds")


def dot(a, b):
    return jnp.dot(a, b, preferred_element_type=F32)


def kernel(
    n_grp, n_dev, levels, cols,
    tr_h, met_h, coef_h, nbr_h, flip_h, send_h, span_h,
    lev_c, lev_b,
    tr_v, met_v, coef_v, nbr_v, flip_v, send_v, span_v,
    send_pos, pos_in, blk_out, blk_in, spread_w,
    edge_w, send_w, edge_out, edge_in, across_v,
    field, first, col_c,
    load_sem, pos_ssem, pos_rsem, blk_ssem, blk_rsem, edge_ssem, edge_rsem,
):
    grp, dev = lax.axis_index("grp"), lax.axis_index("dev")
    points = 16
    per_peer = cols // n_dev
    width = max(per_peer, LANES)
    per_tile = width // LANES
    src_tiles = cols // LANES
    lap = gll_laplacian()

    loads = [
        pltpu.make_async_copy(src, dst, load_sem.at[i])
        for i, (src, dst) in enumerate(
            [(span_h, span_v), (tr_h, tr_v), (send_h, send_v), (coef_h, coef_v),
             (nbr_h, nbr_v), (flip_h, flip_v), (met_h, met_v)]
        )
    ]
    for load in loads:
        load.start()

    barrier = pltpu.get_barrier_semaphore()
    for d in range(1, n_dev):
        pl.semaphore_signal(
            barrier, inc=1, device_id=(grp, lax.rem(dev + d, n_dev)), device_id_type=MESH
        )
    for step in (1, n_grp - 1):
        pl.semaphore_signal(
            barrier, inc=1, device_id=(lax.rem(grp + step, n_grp), dev), device_id_type=MESH
        )

    loads[0].wait()
    span = span_v[...]
    shift = cols.bit_length() - 1
    target = span >> shift
    place = span & (cols - 1)
    hits = jnp.concatenate(
        [jnp.where(target == r, 1.0, 0.0) for r in range(n_dev)], axis=0
    ).astype(BF16)
    count = n_dev * points
    before = one_hot(iota((LANES, LANES), 0) < iota((LANES, LANES), 1))
    along = dot(hits, before)
    totals = dot(hits, jnp.ones((LANES, LANES), BF16))
    row_i, col_i = iota((count, count), 0), iota((count, count), 1)
    earlier = one_hot((col_i < row_i) & ((col_i >> 4) == (row_i >> 4)))
    ranks = along + dot(earlier, totals.astype(BF16))
    rank = jnp.zeros((points, LANES), F32)
    for r in range(n_dev):
        rank = jnp.where(target == r, ranks[r * points:(r + 1) * points], rank)
    rank = rank.astype(I32)
    sub = rank >> 7
    lane = rank & (LANES - 1)
    tile = target * per_tile + sub
    row8 = target * 8 + sub
    place_hi = (place >> 7).astype(F32)
    place_lo = (place & (LANES - 1)).astype(F32)
    rows_out = n_dev * 8
    lists = []
    for p in range(points):
        spread_w[0:LANES, p * LANES:(p + 1) * LANES] = one_hot(
            iota((LANES, LANES), 0) == lane[p:p + 1, :]
        )
        mine = iota((rows_out, LANES), 0) == row8[p:p + 1, :]
        lists.append(
            jnp.concatenate(
                [jnp.where(mine, place_hi[p:p + 1, :], 0.0), jnp.where(mine, place_lo[p:p + 1, :], 0.0)],
                axis=0,
            ).astype(BF16)
        )
    packed = lax.dot_general(
        jnp.concatenate(lists, axis=1),
        spread_w[0:LANES, :],
        (((1,), (1,)), ((), ())),
        preferred_element_type=F32,
    )
    send_pos[...] = packed[:rows_out] * 128.0 + packed[rows_out:]
    edge_in[0, 48:LANES, :] = jnp.zeros((LANES - 48, 3 * LANES), F32)
    edge_in[1, 48:LANES, :] = jnp.zeros((LANES - 48, 3 * LANES), F32)
    send_w[...] = jnp.zeros(send_w.shape, BF16)

    pl.semaphore_wait(barrier, n_dev + 1)

    def pos_copy(peer, slot):
        return pltpu.make_async_remote_copy(
            src_ref=send_pos.at[pl.ds(pl.multiple_of(peer * 8, 8), 8), :],
            dst_ref=pos_in.at[slot],
            send_sem=pos_ssem.at[peer],
            recv_sem=pos_rsem.at[slot],
            device_id=(grp, peer),
            device_id_type=MESH,
        )

    def blk_copy(peer, slot):
        return pltpu.make_async_remote_copy(
            src_ref=blk_out.at[peer],
            dst_ref=blk_in.at[slot],
            send_sem=blk_ssem.at[peer],
            recv_sem=blk_rsem.at[slot],
            device_id=(grp, peer),
            device_id_type=MESH,
        )

    def edge_copies(turn):
        return [
            pltpu.make_async_remote_copy(
                src_ref=edge_out.at[turn, pl.ds(at, rows), :],
                dst_ref=edge_in.at[turn, pl.ds(at, rows), :],
                send_sem=edge_ssem.at[turn, k],
                recv_sem=edge_rsem.at[turn, k],
                device_id=(lax.rem(grp + n_grp + dg, n_grp), lax.rem(dev + n_dev + dv, n_dev)),
                device_id_type=MESH,
            )
            for k, (at, rows, dg, dv) in enumerate(EDGE_ROWS)
        ]

    def far(k):
        return n_dev // 2 + (1 - 2 * (k % 2)) * ((k + 1) // 2)

    def start_pos(k, carry):
        pos_copy(lax.rem(dev + n_dev - far(k), n_dev), dev).start()
        return carry

    lax.fori_loop(0, n_dev - 1, start_pos, 0)

    loads[1].wait()
    loads[2].wait()
    send_w[:, 0:48] = one_hot(iota((4 * LANES, 48), 0) == send_v[...])
    for p in range(points):
        field[p] = tr_v[pl.ds(p, levels, stride=points), :]

    def table_of(ref):
        return halves(
            jnp.concatenate(
                [
                    jnp.concatenate([ref[EDGE_POINT[s][t]] for s in range(4)], axis=1)
                    for t in range(4)
                ],
                axis=0,
            )
        )

    def send_edges(table, turn):
        hi, lo = table
        sent = dot(hi, send_w[...]) + dot(lo, send_w[...])
        rest = jnp.zeros((3 * LANES - 4 * levels, LANES), F32)
        edge_out[turn] = jnp.concatenate([sent, rest], axis=0).T
        for copy in edge_copies(turn):
            copy.start()

    table = table_of(field)
    send_edges(table, 0)

    loads[3].wait()

    def wanted(pos_tile, into):
        pos = pos_tile.astype(I32)
        for k in range(per_tile):
            here = jnp.broadcast_to(pos[k:k + 1, :], (8, LANES))
            low = here & (LANES - 1)
            high = here >> 7
            for at in range(0, levels, 8):
                got = pick(coef_v[at:at + 8, 0:LANES], low)
                for i in range(1, src_tiles):
                    other = pick(coef_v[at:at + 8, i * LANES:(i + 1) * LANES], low)
                    got = jnp.where(high == i, other, got)
                into[at:at + 8, k * LANES:(k + 1) * LANES] = got

    def serve(k, carry):
        peer = lax.rem(dev + far(k), n_dev)
        pos_copy(peer, peer).wait_recv()
        wanted(pos_in[peer], blk_out.at[peer])
        blk_copy(peer, dev).start()
        return carry

    lax.fori_loop(0, n_dev - 1, serve, 0)
    wanted(send_pos[pl.ds(pl.multiple_of(dev * 8, 8), 8), :], blk_in.at[dev])

    for load in loads[4:]:
        load.wait()
    for s in range(4):
        nbr = nbr_v[s:s + 1, :]
        edge_w[:, s * LANES:(s + 1) * LANES] = one_hot(iota((5 * LANES, LANES), 0) == nbr)

    def gather_own(table):
        hi, lo = table
        weights = edge_w[0:4 * LANES, :]
        across_v[...] = dot(hi, weights) + dot(lo, weights)

    def gather_far(turn):
        for copy in edge_copies(turn):
            copy.wait_recv()
        hi, lo = halves(edge_in[turn].T[:4 * levels])
        weights = edge_w[4 * LANES:5 * LANES, :]
        across_v[...] += dot(hi, weights) + dot(lo, weights)

    def operator(ref, emit):
        scale = met_v[...]
        flips = [flip_v[s:s + 1, :] == 1 for s in range(4)]

        def chunk(i, carry):
            at = pl.multiple_of(i * 8, 8)
            u = [ref[p, pl.ds(at, 8), :] for p in range(points)]
            acc = [None] * points
            touch = [0] * points
            for s in range(4):
                for t in range(4):
                    p = EDGE_POINT[s][t]
                    lanes = slice(s * LANES, (s + 1) * LANES)
                    same = across_v[pl.ds(pl.multiple_of(t * levels + at, 8), 8), lanes]
                    back = across_v[pl.ds(pl.multiple_of((3 - t) * levels + at, 8), 8), lanes]
                    value = jnp.where(flips[s], back, same)
                    acc[p] = value if acc[p] is None else acc[p] + value
                    touch[p] += 1
            for p in range(points):
                total = None if acc[p] is None else PENALTY * acc[p]
                for q in range(points):
                    weight = lap[p, q] - (PENALTY * touch[p] if p == q else 0.0)
                    if weight != 0.0:
                        term = np.float32(weight) * u[q]
                        total = term if total is None else total + term
                emit(i, at, p, scale * total)
            return carry

        lax.fori_loop(0, levels // 8, chunk, 0)

    gather_own(table)
    gather_far(0)

    def keep_first(i, at, p, value):
        first[p, pl.ds(at, 8), :] = value

    operator(field, keep_first)
    def arrived(k):
        peer = lax.rem(dev + n_dev - far(k), n_dev)
        blk_copy(peer, peer).wait_recv()
        return peer

    def place_blocks(peers, begin, last):
        for p in range(points):
            low = jnp.broadcast_to(lane[p:p + 1, :], (8, LANES))
            which = jnp.broadcast_to(tile[p:p + 1, :], (8, LANES))
            pairs = [(peer, k, which == peer * per_tile + k) for peer in peers for k in range(per_tile)]
            lanes = slice(p * LANES, (p + 1) * LANES)
            for at in range(0, levels, 8):
                value = None if begin else col_c[at:at + 8, lanes]
                for peer, k, mask in pairs:
                    other = pick(blk_in[peer, at:at + 8, k * LANES:(k + 1) * LANES], low)
                    value = other if value is None else jnp.where(mask, other, value)
                if last:
                    lev_c[pl.ds(at * points + p, 8, stride=points), :] = value
                else:
                    col_c[at:at + 8, lanes] = value

    table = table_of(first)
    send_edges(table, 1)
    gather_own(table)
    place_blocks([dev] + [arrived(k) for k in range(n_dev - 5)], True, False)
    gather_far(1)

    def keep_stepped(i, at, p, value):
        lev_b[pl.ds(i * (8 * points) + p, 8, stride=points), :] = (
            field[p, pl.ds(at, 8), :] - HYPER * value
        )

    operator(first, keep_stepped)
    place_blocks([arrived(k) for k in range(n_dev - 5, n_dev - 3)], False, False)
    place_blocks([arrived(k) for k in range(n_dev - 3, n_dev - 1)], False, True)

    def finish(d, carry):
        peer = lax.rem(dev + d, n_dev)
        pos_copy(peer, dev).wait_send()
        blk_copy(peer, dev).wait_send()
        return carry

    lax.fori_loop(1, n_dev, finish, 0)
    for turn in range(2):
        for copy in edge_copies(turn):
            copy.wait_send()


def solve_kernel(levels, lev_c, lev_b, out, out_v, lev_u, lev_y, sem):
    points = 16

    def level(ref, k):
        return ref[pl.ds(pl.multiple_of(k * points, points), points), :]

    def put(ref, k, value):
        ref[pl.ds(pl.multiple_of(k * points, points), points), :] = value

    mid = levels // 2
    zero = jnp.zeros((points, LANES), F32)
    c_first = level(lev_c, 0)
    batch = 4

    def eliminate(step, carry):
        e, c_up, y, er, u, g, c_dn, z, gr, v = carry
        for part in range(batch):
            k = step * batch + part
            c1 = level(lev_c, k + 1)
            r = pl.reciprocal(e + c1)
            u = c1 * r
            y = (level(lev_b, k) + c_up * y) * r
            er = e * r
            e = 1.0 + c1 * er
            c_up = c1
            put(lev_u, k, u)
            put(lev_y, k, y)
            m = levels - 1 - k
            cm = level(lev_c, m)
            r = pl.reciprocal(g + cm)
            v = cm * r
            z = (level(lev_b, m) + c_dn * z) * r
            gr = g * r
            g = 1.0 + cm * gr
            c_dn = cm
            put(lev_u, m, v)
            put(lev_y, m, z)
        return e, c_up, y, er, u, g, c_dn, z, gr, v

    start = (1.0 + c_first, c_first, zero, zero, zero, zero + 1.0, zero, zero, zero, zero)
    e, c_up, y, er, u, g, c_dn, z, gr, v = lax.fori_loop(0, mid // batch, eliminate, start)
    x_top = (y + u * z) / (er + u * gr)
    x_bot = z + v * x_top
    put(out_v, mid - 1, x_top)
    put(out_v, mid, x_bot)

    def substitute(k, carry):
        x_up, x_dn = carry
        i = mid - 1 - k
        m = mid + k
        x_up = level(lev_y, i) + level(lev_u, i) * x_up
        x_dn = level(lev_y, m) + level(lev_u, m) * x_dn
        put(out_v, i, x_up)
        put(out_v, m, x_dn)
        return x_up, x_dn

    copies = []

    def write(low, high):
        rows = pl.ds(low * points, (high - low) * points)
        copy = pltpu.make_async_copy(out_v.at[rows, :], out.at[rows, :], sem.at[len(copies)])
        copy.start()
        copies.append(copy)

    carry = (x_top, x_bot)
    done = 0
    for k in range(1, mid):
        carry = substitute(k, carry)
        if k % 6 == 5 or k == mid - 1:
            write(mid - 1 - k, mid - done)
            write(mid + done, mid + k + 1)
            done = k + 1
    for copy in copies:
        copy.wait()


def on_device(n_grp, n_dev, tracer, metric, coef, nbr_slot, edge_flip, send_slot, span_slot):
    levels, points, elems = tracer.shape
    cols = coef.shape[1]
    width = max(cols // n_dev, LANES)
    rows = levels * points
    vmem = pltpu.VMEM
    dma = pltpu.SemaphoreType.DMA
    hbm_spec = pl.BlockSpec(memory_space=pltpu.HBM)
    vmem_spec = pl.BlockSpec(memory_space=vmem)
    flat = jax.ShapeDtypeStruct((rows, elems), F32)
    mixing, stepped = pl.pallas_call(
        functools.partial(kernel, n_grp, n_dev, levels, cols),
        out_shape=[flat, flat],
        in_specs=[hbm_spec] * 7,
        out_specs=[vmem_spec, vmem_spec],
        scratch_shapes=[
            vmem((rows, elems), F32),
            vmem((1, elems), F32),
            vmem((levels, cols), F32),
            vmem((4, elems), I32),
            vmem((4, elems), I32),
            vmem((1, 48), I32),
            vmem((points, elems), I32),
            vmem((n_dev * 8, LANES), F32),
            vmem((n_dev, 8, LANES), F32),
            vmem((n_dev, levels, width), F32),
            vmem((n_dev, levels, width), F32),
            vmem((LANES, cols), BF16),
            vmem((5 * LANES, 4 * LANES), BF16),
            vmem((4 * LANES, LANES), BF16),
            vmem((2, LANES, 3 * LANES), F32),
            vmem((2, LANES, 3 * LANES), F32),
            vmem((4 * levels, 4 * LANES), F32),
            vmem((points, levels, elems), F32),
            vmem((points, levels, elems), F32),
            vmem((levels, cols), F32),
            dma((7,)),
            dma((n_dev,)),
            dma((n_dev,)),
            dma((n_dev,)),
            dma((n_dev,)),
            dma((2, 4)),
            dma((2, 4)),
        ],
        compiler_params=pltpu.CompilerParams(
            collective_id=0, has_side_effects=True, vmem_limit_bytes=40 * 2**20
        ),
        cost_estimate=pl.CostEstimate(flops=10**9, bytes_accessed=4 * 10**6, transcendentals=0),
        name="hyper_mix",
    )(
        *[
            pltpu.with_memory_space_constraint(array, pltpu.HBM)
            for array in (
                tracer.reshape(rows, elems),
                metric.reshape(1, elems),
                coef,
                nbr_slot,
                edge_flip,
                send_slot.reshape(1, 48),
                span_slot,
            )
        ]
    )
    mixed = pl.pallas_call(
        functools.partial(solve_kernel, levels),
        out_shape=flat,
        in_specs=[vmem_spec, vmem_spec],
        out_specs=hbm_spec,
        scratch_shapes=[vmem((rows, elems), F32)] * 3 + [dma((2 * (levels // 12 + 1),))],
        compiler_params=pltpu.CompilerParams(vmem_limit_bytes=40 * 2**20),
        cost_estimate=pl.CostEstimate(flops=10**7, bytes_accessed=2 * 10**6, transcendentals=0),
        name="column_solve",
    )(mixing, stepped)
    return mixed.reshape(tracer.shape)


def solution(mesh):
    in_specs = (
        P(None, None, ("grp", "dev")),
        P(("grp", "dev")),
        P(None, ("grp", "dev")),
        P(None, ("grp", "dev")),
        P(None, ("grp", "dev")),
        P(("grp", "dev")),
        P(None, ("grp", "dev")),
    )
    out_specs = P(None, None, ("grp", "dev"))
    body = functools.partial(on_device, mesh.shape["grp"], mesh.shape["dev"])
    return jax.shard_map(body, mesh=mesh, in_specs=in_specs, out_specs=out_specs, check_vma=False)
```

profile of v0, /device:TPU:0, one launch (start us, length us, event | category | flops | bytes accessed | tf_op | source)
XLA Modules:
  0.0 21.8 jit_solution(14441875973610300544)
XLA Ops:
  0.0 20.4 %hyper_mix.1 = (f32[1152,128]{1,0:T(8,128)S(1)}, f32[1152,128]{1,0:T(8,128)S(1)}) custom-call(f32[1152,128]{1,0:T(8,128)} %bitcast.4, f32[1,128]{1,0:T(1,128)} %bitcast.5, f32[72,2048]{1,0:T(8,128)} %coef_h.1, s32[4,128]{1,0:T(4,128)} %nbr_h.1, s32[4,128]{1,0:T(4,128)} %flip_h.1, s32[1,48]{1,0:T(1,128)} %bitcast.6, s32[16,128]{1,0:T(8,128)} %span_h.1), custom_call_target="tpu_custom_call" | custom-call | flops 1000000000 | bytes 4000000 | tf_op jit(solution)/shard_map/hyper_mix/pallas_call | solution.py:439
  20.4 1.3 %column_solve.1 = f32[1152,128]{1,0:T(8,128)} custom-call(f32[1152,128]{1,0:T(8,128)S(1)} %get-tuple-element.7.lev_c, f32[1152,128]{1,0:T(8,128)S(1)} %get-tuple-element.8.lev_b), custom_call_target="tpu_custom_call" | custom-call | flops 10000000 | bytes 2000000 | tf_op jit(solution)/shard_map/column_solve/pallas_call | solution.py:492
where the time goes:
time: 22 us; the launch traced here: 21.8 us
  Pallas kernels  21.8 us (99%)
    pallas_call x1, Pallas kernels, on_device(): pl.pallas_call(functools.partial(kernel, n_grp, n_dev, levels, cols), out...  20.4 us
    pallas_call x1, Pallas kernels, on_device(): pl.pallas_call(functools.partial(solve_kernel, levels), out_shape=flat, i...  1.33 us

commit v1 on v0

--- a/solution.py
+++ b/solution.py
@@ -194,8 +194,8 @@
 
     lax.fori_loop(0, n_dev - 1, start_pos, 0)
 
-    loads[1].wait()
-    loads[2].wait()
+    for load in loads[1:]:
+        load.wait()
     send_w[:, 0:48] = one_hot(iota((4 * LANES, 48), 0) == send_v[...])
     for p in range(points):
         field[p] = tr_v[pl.ds(p, levels, stride=points), :]
@@ -222,33 +222,28 @@
     table = table_of(field)
     send_edges(table, 0)
 
-    loads[3].wait()
-
-    def wanted(pos_tile, into):
-        pos = pos_tile.astype(I32)
+    def wanted(pos, into, at):
         for k in range(per_tile):
             here = jnp.broadcast_to(pos[k:k + 1, :], (8, LANES))
             low = here & (LANES - 1)
             high = here >> 7
-            for at in range(0, levels, 8):
-                got = pick(coef_v[at:at + 8, 0:LANES], low)
-                for i in range(1, src_tiles):
-                    other = pick(coef_v[at:at + 8, i * LANES:(i + 1) * LANES], low)
-                    got = jnp.where(high == i, other, got)
-                into[at:at + 8, k * LANES:(k + 1) * LANES] = got
+            got = pick(coef_v[pl.ds(at, 8), 0:LANES], low)
+            for i in range(1, src_tiles):
+                other = pick(coef_v[pl.ds(at, 8), i * LANES:(i + 1) * LANES], low)
+                got = jnp.where(high == i, other, got)
+            into[pl.ds(at, 8), k * LANES:(k + 1) * LANES] = got
 
     def serve(k, carry):
         peer = lax.rem(dev + far(k), n_dev)
         pos_copy(peer, peer).wait_recv()
-        wanted(pos_in[peer], blk_out.at[peer])
+        pos = pos_in[peer].astype(I32)
+        for at in range(0, levels, 8):
+            wanted(pos, blk_out.at[peer], at)
         blk_copy(peer, dev).start()
         return carry
 
     lax.fori_loop(0, n_dev - 1, serve, 0)
-    wanted(send_pos[pl.ds(pl.multiple_of(dev * 8, 8), 8), :], blk_in.at[dev])
-
-    for load in loads[4:]:
-        load.wait()
+
     for s in range(4):
         nbr = nbr_v[s:s + 1, :]
         edge_w[:, s * LANES:(s + 1) * LANES] = one_hot(iota((5 * LANES, LANES), 0) == nbr)
@@ -265,12 +260,13 @@
         weights = edge_w[4 * LANES:5 * LANES, :]
         across_v[...] += dot(hi, weights) + dot(lo, weights)
 
-    def operator(ref, emit):
+    def operator(ref, emit, beside):
         scale = met_v[...]
         flips = [flip_v[s:s + 1, :] == 1 for s in range(4)]
 
-        def chunk(i, carry):
+        def chunk(i):
             at = pl.multiple_of(i * 8, 8)
+            beside(at)
             u = [ref[p, pl.ds(at, 8), :] for p in range(points)]
             acc = [None] * points
             touch = [0] * points
@@ -291,9 +287,13 @@
                         term = np.float32(weight) * u[q]
                         total = term if total is None else total + term
                 emit(i, at, p, scale * total)
+
+        def chunks(step, carry):
+            for part in range(3):
+                chunk(step * 3 + part)
             return carry
 
-        lax.fori_loop(0, levels // 8, chunk, 0)
+        lax.fori_loop(0, levels // 24, chunks, 0)
 
     gather_own(table)
     gather_far(0)
@@ -301,32 +301,35 @@
     def keep_first(i, at, p, value):
         first[p, pl.ds(at, 8), :] = value
 
-    operator(field, keep_first)
+    own_pos = send_pos[pl.ds(pl.multiple_of(dev * 8, 8), 8), :].astype(I32)
+    operator(field, keep_first, lambda at: wanted(own_pos, blk_in.at[dev], at))
     def arrived(k):
         peer = lax.rem(dev + n_dev - far(k), n_dev)
         blk_copy(peer, peer).wait_recv()
         return peer
 
-    def place_blocks(peers, begin, last):
+    def place_blocks(peers, begin, last, at):
         for p in range(points):
             low = jnp.broadcast_to(lane[p:p + 1, :], (8, LANES))
             which = jnp.broadcast_to(tile[p:p + 1, :], (8, LANES))
-            pairs = [(peer, k, which == peer * per_tile + k) for peer in peers for k in range(per_tile)]
             lanes = slice(p * LANES, (p + 1) * LANES)
-            for at in range(0, levels, 8):
-                value = None if begin else col_c[at:at + 8, lanes]
-                for peer, k, mask in pairs:
-                    other = pick(blk_in[peer, at:at + 8, k * LANES:(k + 1) * LANES], low)
+            value = None if begin else col_c[pl.ds(at, 8), lanes]
+            for peer in peers:
+                for k in range(per_tile):
+                    other = pick(blk_in[peer, pl.ds(at, 8), k * LANES:(k + 1) * LANES], low)
+                    mask = which == peer * per_tile + k
                     value = other if value is None else jnp.where(mask, other, value)
-                if last:
-                    lev_c[pl.ds(at * points + p, 8, stride=points), :] = value
-                else:
-                    col_c[at:at + 8, lanes] = value
+            if last:
+                lev_c[pl.ds(at * points + p, 8, stride=points), :] = value
+            else:
+                col_c[pl.ds(at, 8), lanes] = value
 
     table = table_of(first)
     send_edges(table, 1)
+    peers = [dev] + [arrived(k) for k in range(n_dev - 5)]
     gather_own(table)
-    place_blocks([dev] + [arrived(k) for k in range(n_dev - 5)], True, False)
+    for at in range(0, levels, 8):
+        place_blocks(peers, True, False, at)
     gather_far(1)
 
     def keep_stepped(i, at, p, value):
@@ -334,9 +337,11 @@
             field[p, pl.ds(at, 8), :] - HYPER * value
         )
 
-    operator(first, keep_stepped)
-    place_blocks([arrived(k) for k in range(n_dev - 5, n_dev - 3)], False, False)
-    place_blocks([arrived(k) for k in range(n_dev - 3, n_dev - 1)], False, True)
+    nearer = [arrived(k) for k in range(n_dev - 5, n_dev - 3)]
+    operator(first, keep_stepped, lambda at: place_blocks(nearer, False, False, at))
+    nearest = [arrived(k) for k in range(n_dev - 3, n_dev - 1)]
+    for at in range(0, levels, 8):
+        place_blocks(nearest, False, True, at)
 
     def finish(d, carry):
         peer = lax.rem(dev + d, n_dev)

time: 22 us -> 22.8 us (1.036)
  Pallas kernels: 21.8 us -> 22.5 us
    pallas_call x1, Pallas kernels: 20.4 us -> 21.2 us  [on_device(): pl.pallas_call(functools.partial(kernel, n_grp, n_dev, levels, cols), out...]
where the time goes in v1:
time: 22.8 us; the launch traced here: 22.6 us
  Pallas kernels  22.5 us (99%)
    pallas_call x1, Pallas kernels, on_device(): pl.pallas_call(functools.partial(kernel, n_grp, n_dev, levels, cols), out...  21.2 us
    pallas_call x1, Pallas kernels, on_device(): pl.pallas_call(functools.partial(solve_kernel, levels), out_shape=flat, i...  1.33 us

profile of v1, /device:TPU:0, one launch (start us, length us, event | category | flops | bytes accessed | tf_op | source)
XLA Modules:
  0.0 22.6 jit_solution(1996512974277151943)
XLA Ops:
  0.0 21.2 %hyper_mix.1 = (f32[1152,128]{1,0:T(8,128)S(1)}, f32[1152,128]{1,0:T(8,128)S(1)}) custom-call(f32[1152,128]{1,0:T(8,128)} %bitcast.4, f32[1,128]{1,0:T(1,128)} %bitcast.5, f32[72,2048]{1,0:T(8,128)} %coef_h.1, s32[4,128]{1,0:T(4,128)} %nbr_h.1, s32[4,128]{1,0:T(4,128)} %flip_h.1, s32[1,48]{1,0:T(1,128)} %bitcast.6, s32[16,128]{1,0:T(8,128)} %span_h.1), custom_call_target="tpu_custom_call" | custom-call | flops 1000000000 | bytes 4000000 | tf_op jit(solution)/shard_map/hyper_mix/pallas_call | solution.py:444
  21.2 1.3 %column_solve.1 = f32[1152,128]{1,0:T(8,128)} custom-call(f32[1152,128]{1,0:T(8,128)S(1)} %get-tuple-element.7.lev_c, f32[1152,128]{1,0:T(8,128)S(1)} %get-tuple-element.8.lev_b), custom_call_target="tpu_custom_call" | custom-call | flops 10000000 | bytes 2000000 | tf_op jit(solution)/shard_map/column_solve/pallas_call | solution.py:497

commit v2 on v0

--- a/solution.py
+++ b/solution.py
@@ -68,7 +68,7 @@
     tr_h, met_h, coef_h, nbr_h, flip_h, send_h, span_h,
     lev_c, lev_b,
     tr_v, met_v, coef_v, nbr_v, flip_v, send_v, span_v,
-    send_pos, pos_in, blk_out, blk_in, spread_w,
+    send_pos, pos_in, stack, blk_out, blk_in, spread_w,
     edge_w, send_w, edge_out, edge_in, across_v,
     field, first, col_c,
     load_sem, pos_ssem, pos_rsem, blk_ssem, blk_rsem, edge_ssem, edge_rsem,
@@ -224,18 +224,37 @@
 
     loads[3].wait()
 
+    by_dot = levels // 2 // 16 * 16
+    coef_hi, coef_lo = halves(
+        jnp.concatenate(
+            [coef_v[0:by_dot, i * LANES:(i + 1) * LANES] for i in range(src_tiles)], axis=0
+        )
+    )
+    stack[:, 0:LANES] = coef_hi
+    stack[:, LANES:2 * LANES] = coef_lo
+
     def wanted(pos_tile, into):
         pos = pos_tile.astype(I32)
+        row = jnp.concatenate([pos[k:k + 1, :] for k in range(per_tile)], axis=1)
+        chosen = one_hot(iota((LANES, width), 0) == (row & (LANES - 1)))
+        all_tiles = dot(stack[...], jnp.concatenate([chosen, chosen], axis=0))
         for k in range(per_tile):
             here = jnp.broadcast_to(pos[k:k + 1, :], (8, LANES))
             low = here & (LANES - 1)
-            high = here >> 7
-            for at in range(0, levels, 8):
+            masks = [(here >> 7) == i for i in range(src_tiles)]
+            for at in range(by_dot, levels, 8):
                 got = pick(coef_v[at:at + 8, 0:LANES], low)
                 for i in range(1, src_tiles):
                     other = pick(coef_v[at:at + 8, i * LANES:(i + 1) * LANES], low)
-                    got = jnp.where(high == i, other, got)
+                    got = jnp.where(masks[i], other, got)
                 into[at:at + 8, k * LANES:(k + 1) * LANES] = got
+            for at in range(0, by_dot, 8):
+                lanes = slice(k * LANES, (k + 1) * LANES)
+                got = all_tiles[at:at + 8, lanes]
+                for i in range(1, src_tiles):
+                    other = all_tiles[i * by_dot + at:i * by_dot + at + 8, lanes]
+                    got = jnp.where(masks[i], other, got)
+                into[at:at + 8, lanes] = got
 
     def serve(k, carry):
         peer = lax.rem(dev + far(k), n_dev)
@@ -451,6 +470,7 @@
             vmem((points, elems), I32),
             vmem((n_dev * 8, LANES), F32),
             vmem((n_dev, 8, LANES), F32),
+            vmem((cols // LANES * (levels // 2 // 16 * 16), 2 * LANES), BF16),
             vmem((n_dev, levels, width), F32),
             vmem((n_dev, levels, width), F32),
             vmem((LANES, cols), BF16),

time: 22 us -> 21.7 us (0.986)
  Pallas kernels: 21.8 us -> 21.5 us
    pallas_call x1, Pallas kernels: 20.4 us -> 20.2 us  [on_device(): pl.pallas_call(functools.partial(kernel, n_grp, n_dev, levels, cols), out...]
where the time goes in v2:
time: 21.7 us; the launch traced here: 21.5 us
  Pallas kernels  21.5 us (99%)
    pallas_call x1, Pallas kernels, on_device(): pl.pallas_call(functools.partial(kernel, n_grp, n_dev, levels, cols), out...  20.2 us
    pallas_call x1, Pallas kernels, on_device(): pl.pallas_call(functools.partial(solve_kernel, levels), out_shape=flat, i...  1.33 us

profile of v2, /device:TPU:0, one launch (start us, length us, event | category | flops | bytes accessed | tf_op | source)
XLA Modules:
  0.0 21.5 jit_solution(1594817637867692709)
XLA Ops:
  0.0 20.2 %hyper_mix.1 = (f32[1152,128]{1,0:T(8,128)S(1)}, f32[1152,128]{1,0:T(8,128)S(1)}) custom-call(f32[1152,128]{1,0:T(8,128)} %bitcast.4, f32[1,128]{1,0:T(1,128)} %bitcast.5, f32[72,2048]{1,0:T(8,128)} %coef_h.1, s32[4,128]{1,0:T(4,128)} %nbr_h.1, s32[4,128]{1,0:T(4,128)} %flip_h.1, s32[1,48]{1,0:T(1,128)} %bitcast.6, s32[16,128]{1,0:T(8,128)} %span_h.1), custom_call_target="tpu_custom_call" | custom-call | flops 1000000000 | bytes 4000000 | tf_op jit(solution)/shard_map/hyper_mix/pallas_call | solution.py:458
  20.2 1.3 %column_solve.1 = f32[1152,128]{1,0:T(8,128)} custom-call(f32[1152,128]{1,0:T(8,128)S(1)} %get-tuple-element.7.lev_c, f32[1152,128]{1,0:T(8,128)S(1)} %get-tuple-element.8.lev_b), custom_call_target="tpu_custom_call" | custom-call | flops 10000000 | bytes 2000000 | tf_op jit(solution)/shard_map/column_solve/pallas_call | solution.py:512
